TPU v7x, 32 devices: a whole 2x2x4 slice. The times are simulated.
32 devices in a mesh: leaf: 8 (over z, core), vec: 4 (over y, x).
Axes of the slice: x: 2, y: 2, z: 4, core: 2. Of those that a mesh axis runs over, the one named last changes fastest.
Arguments:
- points: bfloat16 [128, 3, 256], P('leaf'), may hold values from 0 to 1
- probe_vectors: bfloat16 [128, 256, 256], P('leaf', 'vec'), may hold values from -6 to 6
- neighbours: int32 [128, 16], P('leaf'), may hold values from -1 to 127, as said below
- leaf_pivots: int32 [128, 64], P('leaf'), may hold values from 0 to 255, as said below
- leaf_inverse: float32 [128, 64, 64], P('leaf'), as said below
- local_pivots: int32 [120, 64], P('leaf'), may hold values from 0 to 127, as said below
- local_inverse: float32 [120, 64, 64], P('leaf'), as said below
- upper_pivots: int32 [7, 64], replicated, may hold values from 0 to 127, as said below
- upper_inverse: float32 [7, 64, 64], replicated, as said below
Outputs:
- leaf_interp: float32 [128, 256, 64], P('leaf')
- local_interp: float32 [120, 128, 64], P('leaf')
- upper_interp: float32 [8, 3, 128, 64], P('leaf')
- top_sketch: float32 [8, 256, 64], P('leaf', 'vec')
Inputs may be any that keep to these rules, and one draw needn't show every extreme that they name: Entry 0 of neighbours[i] is i; then come distinct clusters j != i with |j - i| <= 16, then -1 to the end. The first cluster of each group of 16 lists the cluster before it in entry 1, and the last one lists the cluster after it there, where those exist. A list holds at least 4 clusters, and some lists hold 16. `leaf_pivots`: each row holds 64 distinct row numbers. `local_pivots`: each row holds 64 distinct row numbers. `upper_pivots`: each row holds 64 distinct row numbers. `leaf_inverse`: diagonal entries lie in 0.5 to 1.5. `local_inverse`: diagonal entries lie in 0.5 to 1.5. `upper_inverse`: diagonal entries lie in 0.5 to 1.5.
All inputs are finite; a program needn't handle non-finite values.
Results may differ from a plain program's by a relative error of at most 0.0013.
Values may be sent and summed in bfloat16 or wider, within the bound.
No kernel may reach another device: no remote copies, remote signals or barrier semaphores. Data moves between devices by JAX's collectives and lax.ppermute only.
A program may use at most 64 MiB of HBM per device.

v0:
```python
import functools

import jax
import jax.numpy as jnp
from jax import lax
from jax.experimental import pallas as pl
from jax.experimental.pallas import tpu as pltpu
from jax.sharding import PartitionSpec as P

UPL = 3

SOFTEN = 0.0009
EPSILON = 1e-06
FLIGHT = 8
DEPTH = 128
ROUND_FLOPS = 850_000_000
VMEM_BYTES = 20 * 1024 * 1024
VMEM = pltpu.MemorySpace.VMEM
SMEM = pltpu.MemorySpace.SMEM


def nt(a, b):
    return lax.dot_general(a, b, (((1,), (1,)), ((), ())), preferred_element_type=jnp.float32)


def nn(a, b):
    return lax.dot_general(a, b, (((1,), (0,)), ((), ())), preferred_element_type=jnp.float32)


def split(a):
    high = a.astype(jnp.bfloat16)
    low = (a - high.astype(jnp.float32)).astype(jnp.bfloat16)
    return high, low


def stacked_split(a):
    high, low = split(a)
    return jnp.concatenate([high, low], axis=0)


def halves(a):
    rows = a.shape[0] // 2
    return a[:rows] + a[rows:]


def coordinates(points, extra):
    row = lax.broadcasted_iota(jnp.int32, (8, points.shape[1]), 0)
    padded = jnp.concatenate(
        [points, jnp.full((5, points.shape[1]), 0.5, jnp.float32)], axis=0
    )
    centred = padded - 0.5
    high, low = [part.astype(jnp.float32) for part in split(centred)]
    norm = jnp.sum(centred * centred, axis=0, keepdims=True) + extra
    first, rest = [part.astype(jnp.float32) for part in split(norm)]
    second, third = [part.astype(jnp.float32) for part in split(norm - first)]
    norms = jnp.where(row == 0, first, jnp.where(row == 1, second, jnp.where(row == 2, third, 0.0)))
    return high, low, norms, jnp.where(row < 3, 1.0, 0.0)


def far_features(points):
    high, low, norm, one = coordinates(points, SOFTEN)
    vacant = jnp.zeros((DEPTH - 48, points.shape[1]), jnp.float32)
    return jnp.concatenate(
        [-2.0 * high, -2.0 * low, -2.0 * high, -2.0 * low, one, norm, vacant], axis=0
    ).astype(jnp.bfloat16)


def near_features(points):
    high, low, norm, one = coordinates(points, 0.0)
    vacant = jnp.zeros((DEPTH - 48, points.shape[1]), jnp.float32)
    return jnp.transpose(
        jnp.concatenate([high, high, low, low, norm, one, vacant], axis=0)
    ).astype(jnp.bfloat16)


def add_blocks(share, tiers, base, wanted, nb_ref, far, vectors, near, total, tiles, codes):
    me = lax.axis_index("vec")
    count, slots = nb_ref.shape
    first = lax.axis_index("leaf") * count
    flight, size = tiles.shape[0], tiles.shape[1]
    idle = count * 64

    for way in range(flight):
        codes[way] = idle
    filled = jnp.int32(flight)
    for tier in tiers:
        for part in range(share):
            cluster = (me ^ tier) * share + part
            for slot in range(slots):
                listed = nb_ref[cluster, slot]
                position = listed - first + count
                codes[filled] = cluster * 64 + position - base
                filled += ((listed >= 0) & wanted(position, count)).astype(jnp.int32)
    for way in range(flight):
        codes[filled + way] = idle
    tiles[...] = jnp.zeros(tiles.shape, tiles.dtype)

    def multiply(code, tile):
        row = code // 64
        total[row] = total[row] + nt(vectors[code % 64], tile[...])

    def evaluate(code, tile):
        row = code // 64
        position = code % 64
        for top in range(0, size, 128):
            distance = nn(near[row, top : top + 128, :], far[position])
            tile[top : top + 128, :] = jnp.exp2(-0.5 * jnp.log2(distance)).astype(
                jnp.bfloat16
            )

    def step(index, carry):
        for way in range(flight):
            multiply(codes[index * flight + way], tiles.at[way])
            evaluate(codes[(index + 1) * flight + way], tiles.at[way])
        return carry

    steps = (filled - 1) // flight
    lax.fori_loop(0, steps, step, 0)
    for way in range(flight):
        multiply(codes[steps * flight + way], tiles.at[way])


def inside(position, count):
    return (position >= count) & (position < 2 * count)


def outside(position, count):
    return (position < count) | (position >= 2 * count)


def anywhere(position, count):
    return position >= 0


def own_kernel(share, tiers, nb_ref, points, probe, total, far, near, tiles, codes):
    count = points.shape[0]
    for cluster in range(count):
        here = points[cluster].astype(jnp.float32)
        far[cluster] = far_features(here)
        near[cluster] = near_features(here)
    near[count] = near[0]
    total[...] = jnp.zeros(total.shape, total.dtype)
    add_blocks(share, tiers, count, inside, nb_ref, far, probe, near, total, tiles, codes)


def halo_kernel(share, tiers, nb_ref, probe, before, after, own_far, near, start, *refs):
    outs = refs[: len(tiers)]
    far, vectors, total, tiles, codes = refs[len(tiers) :]
    count, columns, _ = probe.shape
    me = lax.axis_index("vec")
    for place, source in ((0, before), (2, after)):
        for cluster in range(count):
            far[place * count + cluster] = far_features(
                source[cluster, columns:, :].astype(jnp.float32)[0:3]
            )
        vectors[place * count : (place + 1) * count] = source[:, 0:columns, :]
    far[count : 2 * count] = own_far[...]
    vectors[count : 2 * count] = probe[...]
    total[...] = start[...]
    add_blocks(share, tiers, 0, outside, nb_ref, far, vectors, near, total, tiles, codes)
    for tier, out in zip(tiers, outs):
        part = total[pl.ds((me ^ tier) * share, share)]
        out[...] = (part * 0.015625).astype(out.dtype)


def kept_kernel(share, nb_ref, far, vectors, near, out, total, tiles, codes):
    mine = pl.ds(lax.axis_index("vec") * share, share)
    total[mine] = jnp.zeros((share,) + total.shape[1:], total.dtype)
    add_blocks(share, (0,), 0, anywhere, nb_ref, far, vectors, near, total, tiles, codes)
    out[...] = (total[mine] * 0.015625).astype(out.dtype)


def join_kernel(points, probe, joined):
    count, columns, size = probe.shape
    joined[:, 0:columns, :] = probe[...]
    vacant = jnp.zeros((joined.shape[1] - columns - 3, size), jnp.float32)
    for cluster in range(count):
        joined[cluster, columns:, :] = jnp.concatenate(
            [points[cluster].astype(jnp.float32), vacant], axis=0
        ).astype(joined.dtype)


def near_call(body, outs, scratch, operands, rows, per_row):
    nb, size = operands[0], outs[0].shape[-1]
    blocks = rows * per_row
    return pl.pallas_call(
        body,
        out_shape=outs,
        in_specs=[pl.BlockSpec(memory_space=SMEM)]
        + [pl.BlockSpec(memory_space=VMEM)] * (len(operands) - 1),
        out_specs=[pl.BlockSpec(memory_space=VMEM)] * len(outs),
        scratch_shapes=scratch
        + [
            pltpu.VMEM((FLIGHT, size, size), jnp.bfloat16),
            pltpu.SMEM((rows * nb.shape[1] + 2 * FLIGHT,), jnp.int32),
        ],
        compiler_params=pltpu.CompilerParams(vmem_limit_bytes=VMEM_BYTES),
        cost_estimate=pl.CostEstimate(
            flops=blocks * size * size * 256,
            bytes_accessed=sum(o.size * o.dtype.itemsize for o in operands),
            transcendentals=blocks * size * size,
        ),
    )(*operands)


def pivot_factor(pivots, inverse, width):
    chosen = (
        lax.broadcasted_iota(jnp.int32, (width, pivots.shape[1]), 0) == pivots
    ).astype(jnp.bfloat16)
    return nt(stacked_split(jnp.transpose(inverse)), chosen).astype(jnp.bfloat16)


def leaf_node(sketch, pivots, inverse):
    factor = pivot_factor(pivots, inverse, sketch.shape[1])
    wide = sketch.astype(jnp.float32)
    mean_sq = jnp.sum(wide * wide, keepdims=True) / (sketch.shape[0] * sketch.shape[1]) + EPSILON
    scale = 1.0 / (sketch.shape[0] * mean_sq)
    picked = halves(nt(factor, sketch))
    raw = halves(nn(stacked_split(picked), sketch))
    interp = raw * scale
    upward = halves(nt(stacked_split(raw), sketch)) * (scale * lax.rsqrt(mean_sq))
    return interp, upward


def tree_node(sketch, pivots, inverse):
    width, columns = sketch.shape
    factor = pivot_factor(pivots, inverse, width)
    mean_sq = jnp.sum(sketch * sketch, keepdims=True) / (width * columns) + EPSILON
    scale = 1.0 / (columns * mean_sq)
    parts = stacked_split(sketch)
    picked = halves(nn(jnp.concatenate([factor, factor], axis=1), parts))
    raw = halves(nt(stacked_split(picked), parts))
    raw = raw[:, :width] + raw[:, width:]
    interp = raw * scale
    both = stacked_split(raw)
    upward = halves(nn(jnp.concatenate([both, both], axis=1), parts)) * (scale * lax.rsqrt(mean_sq))
    return interp, upward


def device_kernel(
    share,
    group,
    rank,
    own,
    *refs,
):
    parts = group // share
    arrived = refs[: parts - 1]
    pivots, inverse, local_pivots, local_inverse, pack, up_out, sketch, ups = refs[parts - 1 :]
    me = lax.axis_index("vec")
    columns = own.shape[1]
    size = own.shape[2]
    for tier, piece in enumerate((own,) + tuple(arrived)):
        place = pl.ds(pl.multiple_of((me ^ tier) * columns, columns), columns)
        for cluster in range(share):
            sketch[cluster, place, :] = piece[cluster]
    for cluster in range(share):
        row = me * share + cluster
        interp, upward = leaf_node(sketch[cluster], pivots[pl.ds(row, 1), :], inverse[row])
        pack[cluster * rank : (cluster + 1) * rank, :] = interp
        ups[cluster * rank : (cluster + 1) * rank, :] = upward
    level_first, nodes, packed = 0, share // 2, 0
    level_nodes = group // 2
    while nodes >= 1:
        results = []
        for node in range(nodes):
            row = level_first + me * nodes + node
            interp, upward = tree_node(
                ups[2 * node * rank : 2 * (node + 1) * rank, :],
                local_pivots[pl.ds(row, 1), :],
                local_inverse[row],
            )
            top = (share + packed // 2) * rank
            side = (packed % 2) * 2 * rank
            pack[top : top + rank, side : side + 2 * rank] = interp
            results.append(upward)
            packed += 1
        for node, upward in enumerate(results):
            ups[node * rank : (node + 1) * rank, :] = upward
        level_first += level_nodes
        level_nodes //= 2
        nodes //= 2
    up_out[...] = ups[0:rank, :]


def group_kernel(share, group, rank, own, *refs):
    parts = group // share
    arrived = refs[: parts - 1]
    local_pivots, local_inverse, interps, up_out, ups = refs[parts - 1 :]
    me = lax.axis_index("vec")
    for tier, piece in enumerate((own,) + tuple(arrived)):
        ups[pl.ds(pl.multiple_of((me ^ tier) * rank, rank), rank), :] = piece[...]
    row = group - parts
    done = 0
    nodes = parts // 2
    while nodes >= 1:
        results = []
        for node in range(nodes):
            interp, upward = tree_node(
                ups[2 * node * rank : 2 * (node + 1) * rank, :],
                local_pivots[row : row + 1, :],
                local_inverse[row],
            )
            interps[done] = interp
            results.append(upward)
            row += 1
            done += 1
        for node, upward in enumerate(results):
            ups[node * rank : (node + 1) * rank, :] = upward
        nodes //= 2
    up_out[...] = ups[0:rank, :]


def upper_kernel(tier, heap_first, last, rank, own, arrived, pivots, inverse, *refs):
    refs = list(refs)
    if last:
        earlier = [refs.pop(0) for _ in range(tier)]
        interps, top, ups, turned = refs
    else:
        interp_out, up_out, ups = refs
    me = lax.axis_index("leaf")
    side = (me >> tier) & 1
    ups[pl.ds(pl.multiple_of(side * rank, rank), rank), :] = own[...]
    ups[pl.ds(pl.multiple_of((1 - side) * rank, rank), rank), :] = arrived[...]
    node = heap_first + (me >> (tier + 1))
    interp, upward = tree_node(ups[...], pivots[pl.ds(node, 1), :], inverse[node])
    if last:
        for index, ref in enumerate(earlier):
            interps[index] = ref[...]
        interps[tier] = interp
        turned[...] = jnp.transpose(upward)
        columns = top.shape[0]
        place = lax.axis_index("vec") * columns
        top[...] = turned[pl.ds(pl.multiple_of(place, columns), columns), :]
    else:
        interp_out[...] = interp
        up_out[...] = upward


def place_kernel(share, group, rank, own, *refs):
    parts = group // share
    arrived = refs[: parts - 1]
    joined, leaf_out, local_out = refs[parts - 1 :]
    me = lax.axis_index("vec")
    for tier, piece in enumerate((own,) + tuple(arrived)):
        device = me ^ tier
        for cluster in range(share):
            leaf_out[device * share + cluster] = piece[cluster * rank : (cluster + 1) * rank, :]
        level_first, nodes, packed = 0, share // 2, 0
        level_nodes = group // 2
        while nodes >= 1:
            for node in range(nodes):
                top = (share + packed // 2) * rank
                side = (packed % 2) * 2 * rank
                local_out[level_first + device * nodes + node] = piece[
                    top : top + rank, side : side + 2 * rank
                ]
                packed += 1
            level_first += level_nodes
            level_nodes //= 2
            nodes //= 2
    for index in range(parts - 1):
        local_out[group - parts + index] = joined[index]


def call(body, outs, scratch, operands, flops=0):
    return pl.pallas_call(
        body,
        out_shape=outs,
        in_specs=[pl.BlockSpec(memory_space=VMEM)] * len(operands),
        out_specs=jax.tree.map(lambda _: pl.BlockSpec(memory_space=VMEM), outs),
        scratch_shapes=scratch,
        compiler_params=pltpu.CompilerParams(vmem_limit_bytes=VMEM_BYTES),
        cost_estimate=pl.CostEstimate(
            flops=flops, bytes_accessed=sum(o.size * o.dtype.itemsize for o in operands), transcendentals=0
        ),
    )(*operands)


def f32(*shape):
    return jax.ShapeDtypeStruct(shape, jnp.float32)


def on_device(
    points,
    probe_vectors,
    neighbours,
    leaf_pivots,
    leaf_inverse,
    local_pivots,
    local_inverse,
    upper_pivots,
    upper_inverse,
):
    group, columns, size = probe_vectors.shape
    rank = leaf_pivots.shape[1]
    leaf_total = lax.axis_size("leaf")
    parts = lax.axis_size("vec")
    share = group // parts
    total_columns = columns * parts

    up = [(i, i + 1) for i in range(leaf_total - 1)]
    down = [(j, i) for i, j in up]
    joined = call(
        join_kernel,
        jax.ShapeDtypeStruct((group, columns + 16, size), jnp.bfloat16),
        [],
        [points, probe_vectors],
    )
    halo = (lax.ppermute(joined, "leaf", up), lax.ppermute(joined, "leaf", down))

    def vec_send(array, tier):
        return lax.ppermute(array, "vec", [(i, i ^ tier) for i in range(parts)])

    away = list(range(parts - 1, 0, -1))
    sent_rows = (parts - 1) * share

    def bf16(*shape):
        return jax.ShapeDtypeStruct(shape, jnp.bfloat16)

    started, own_far, near = near_call(
        functools.partial(own_kernel, share, away),
        [f32(group + 1, columns, size), bf16(group, DEPTH, size), bf16(group + 1, size, DEPTH)],
        [],
        [neighbours, points, probe_vectors],
        sent_rows,
        6,
    )
    *sent, far, vectors = near_call(
        functools.partial(halo_kernel, share, away),
        [bf16(share, columns, size)] * len(away)
        + [bf16(3 * group, DEPTH, size), bf16(3 * group, columns, size)],
        [pltpu.VMEM((group + 1, columns, size), jnp.float32)],
        [neighbours, probe_vectors, *halo, own_far, near, started],
        sent_rows,
        6,
    )
    arrived = {tier: vec_send(array, tier) for tier, array in zip(away, sent)}
    kept = near_call(
        functools.partial(kept_kernel, share),
        [bf16(share, columns, size)],
        [pltpu.VMEM((group + 1, columns, size), jnp.float32)],
        [neighbours, far, vectors, near],
        share,
        12,
    )[0]

    pack_rows = share * rank + (share // 2) * rank
    pack, own_up = call(
        functools.partial(device_kernel, share, group, rank),
        (f32(pack_rows, size), f32(rank, total_columns)),
        [
            pltpu.VMEM((share, total_columns, size), jnp.bfloat16),
            pltpu.VMEM((share * rank, total_columns), jnp.float32),
        ],
        [kept]
        + [arrived[tier] for tier in range(1, parts)]
        + [leaf_pivots, leaf_inverse, local_pivots, local_inverse],
    )
    near_ups = [vec_send(own_up, tier) for tier in range(1, parts)]
    joined, own_up = call(
        functools.partial(group_kernel, share, group, rank),
        (f32(parts - 1, rank, 2 * rank), f32(rank, total_columns)),
        [pltpu.VMEM((parts * rank, total_columns), jnp.float32)],
        [own_up] + near_ups + [local_pivots, local_inverse],
    )

    pack, own_up = lax.optimization_barrier((pack, own_up))
    others = [vec_send(pack, tier) for tier in range(1, parts)]

    heap_first = 0
    maps = []
    for tier in range(UPL):
        last = tier == UPL - 1
        partner = lax.ppermute(own_up, "leaf", [(i, i ^ (1 << tier)) for i in range(leaf_total)])
        outs = (f32(rank, 2 * rank), f32(rank, total_columns))
        scratch = [pltpu.VMEM((2 * rank, total_columns), jnp.float32)]
        operands = [own_up, partner, upper_pivots, upper_inverse]
        if last:
            outs = (f32(UPL, rank, 2 * rank), f32(columns, rank))
            scratch.append(pltpu.VMEM((total_columns, rank), jnp.float32))
            operands += maps
        first, own_up = call(
            functools.partial(upper_kernel, tier, heap_first, last, rank),
            outs,
            scratch,
            operands,
            flops=ROUND_FLOPS,
        )
        maps.append(first)
        heap_first += leaf_total >> (tier + 1)
    leaf_map, local_map = call(
        functools.partial(place_kernel, share, group, rank),
        (f32(group, rank, size), f32(group - 1, rank, 2 * rank)),
        [],
        [pack] + others + [joined],
    )
    return (
        jnp.swapaxes(leaf_map, 1, 2),
        jnp.swapaxes(local_map, 1, 2),
        jnp.swapaxes(first, 1, 2)[None],
        own_up[None],
    )


def solution(mesh):
    placed = (
        P("leaf", None, None),
        P("leaf", "vec", None),
        P("leaf", None),
        P("leaf", None),
        P("leaf", None, None),
        P("leaf", None),
        P("leaf", None, None),
        P(),
        P(),
    )
    return jax.shard_map(
        on_device,
        mesh=mesh,
        in_specs=placed,
        out_specs=(
            P("leaf", None, None),
            P("leaf", None, None),
            P("leaf", None, None, None),
            P("leaf", "vec", None),
        ),
        check_vma=False,
    )
```

profile of v0, /device:TPU:0, one launch (start us, length us, event | category | flops | bytes accessed | tf_op | source)
XLA Modules:
  0.0 69.7 jit_solution(12514627682572415261)
XLA Ops:
  0.6 0.8 %copy.13.points = bf16[16,3,256]{2,1,0:T(4,128)(2,1)S(1)} copy(bf16[16,3,256]{2,0,1:T(8,128)(2,1)} %param.9) | data formatting | bytes 49152 | tf_op args[0]
  1.4 0.0 copy-start.2
  1.4 1.0 %copy-done.2 = bf16[16,64,256]{2,1,0:T(8,128)(2,1)S(1)} copy-done((bf16[16,64,256]{2,1,0:T(8,128)(2,1)S(1)}, bf16[16,64,256]{2,1,0:T(8,128)(2,1)}, u32[]{:S(2)}) %copy-start.2) | copy-done | bytes 524312
  2.4 0.0 copy-start.6
  2.5 0.0 copy-start.3
  2.5 1.4 %collective-permute-start.1 = (bf16[16,80,256]{2,1,0:T(8,128)(2,1)S(1)}, bf16[16,80,256]{2,1,0:T(8,128)(2,1)S(1)}, u32[]{:S(2)}, u32[]{:S(2)}) collective-permute-start(bf16[16,80,256]{2,1,0:T(8,128)(2,1)S(1)} %shard_map.120), channel_id=1, source_target_pairs={{4,0},{8,4},{12,8},{16,12},{20,16},{24,20},{28,24},{5,1},{9,5},{13... | collective-permute-start | bytes 1966088 | tf_op jit(solution)/shard_map/ppermute | solution.py:410
  3.9 3.1 %collective-permute-start = (bf16[16,80,256]{2,1,0:T(8,128)(2,1)S(1)}, bf16[16,80,256]{2,1,0:T(8,128)(2,1)S(1)}, u32[]{:S(2)}, u32[]{:S(2)}) collective-permute-start(bf16[16,80,256]{2,1,0:T(8,128)(2,1)S(1)} %shard_map.120), channel_id=1, source_target_pairs={{0,4},{4,8},{8,12},{12,16},{16,20},{20,24},{24,28},{1,5},{5,9},{9,... | collective-permute-start | bytes 1966088 | tf_op jit(solution)/shard_map/ppermute | solution.py:410
  7.0 0.0 copy-start.5
  7.0 0.7 copy-done.5
  7.7 11.2 %shard_map.121 = (f32[17,64,256]{2,1,0:T(8,128)S(1)}, bf16[16,128,256]{2,1,0:T(8,128)(2,1)S(1)}, bf16[17,256,128]{2,1,0:T(8,128)(2,1)S(1)}) custom-call(s32[16,16]{1,0:T(8,128)S(1)} %copy-done.5, bf16[16,3,256]{2,1,0:T(4,128)(2,1)S(1)} %copy.13.points, bf16[16,64,256]{2,1,0:T(8,128)(2,1)S(1)} %copy-done.2), custom_call_target="tpu_custom_call" | custom-call | flops 1207959552 | bytes 549888 | tf_op jit(solution)/shard_map/pallas_call | solution.py:186
  18.9 0.0 collective-permute-done.1.after
  19.0 0.0 collective-permute-done.before
  19.0 0.0 copy-done.6
  19.0 0.0 copy-done.3
  19.0 7.3 %shard_map.122 = (bf16[4,64,256]{2,1,0:T(8,128)(2,1)S(1)}, bf16[4,64,256]{2,1,0:T(8,128)(2,1)S(1)}, bf16[4,64,256]{2,1,0:T(8,128)(2,1)S(1)}, bf16[48,128,256]{2,1,0:T(8,128)(2,1)S(1)}, bf16[48,64,256]{2,1,0:T(8,128)(2,1)S(1)}) custom-call(s32[16,16]{1,0:T(8,128)S(1)} %copy-done.6, bf16[16,64,256]{2,1,0:T(8,128)(2,1)S(1)} %copy-done.3, ...), custom_call_target="tpu_custom_call" | custom-call | flops 1207959552 | bytes 5112832 | tf_op jit(solution)/shard_map/pallas_call | solution.py:186
  26.3 2.3 %collective-permute-start.2 = (bf16[4,64,256]{2,1,0:T(8,128)(2,1)S(1)}, bf16[4,64,256]{2,1,0:T(8,128)(2,1)S(1)}, u32[]{:S(2)}, u32[]{:S(2)}) collective-permute-start(bf16[4,64,256]{2,1,0:T(8,128)(2,1)S(1)} %get-tuple-element.31), channel_id=1, source_target_pairs={{0,1},{1,0},{2,3},{3,2},{4,5},{5,4},{6,7},{7,6},{8,9},{9,8},{10,11... | collective-permute-start | bytes 393224 | tf_op jit(solution)/shard_map/ppermute | solution.py:413
  28.6 0.8 %collective-permute-start.3 = (bf16[4,64,256]{2,1,0:T(8,128)(2,1)S(1)}, bf16[4,64,256]{2,1,0:T(8,128)(2,1)S(1)}, u32[]{:S(2)}, u32[]{:S(2)}) collective-permute-start(bf16[4,64,256]{2,1,0:T(8,128)(2,1)S(1)} %get-tuple-element.32), channel_id=1, source_target_pairs={{0,2},{1,3},{2,0},{3,1},{4,6},{5,7},{6,4},{7,5},{8,10},{9,11},{10,... | collective-permute-start | bytes 393224 | tf_op jit(solution)/shard_map/ppermute | solution.py:413
  29.3 0.8 %collective-permute-start.4 = (bf16[4,64,256]{2,1,0:T(8,128)(2,1)S(1)}, bf16[4,64,256]{2,1,0:T(8,128)(2,1)S(1)}, u32[]{:S(2)}, u32[]{:S(2)}) collective-permute-start(bf16[4,64,256]{2,1,0:T(8,128)(2,1)S(1)} %get-tuple-element.33), channel_id=1, source_target_pairs={{0,3},{1,2},{2,1},{3,0},{4,7},{5,6},{6,5},{7,4},{8,11},{9,10},{10,... | collective-permute-start | bytes 393224 | tf_op jit(solution)/shard_map/ppermute | solution.py:413
  30.1 0.0 copy-start
  30.1 0.0 copy-start.1
  30.1 0.0 copy-start.4
  30.1 0.0 copy-start.7
  30.1 5.9 %shard_map.123.own = bf16[4,64,256]{2,1,0:T(8,128)(2,1)S(1)} custom-call(s32[16,16]{1,0:T(8,128)S(1)} %copy-done.6, bf16[48,128,256]{2,1,0:T(8,128)(2,1)S(1)} %get-tuple-element.29.far, bf16[48,64,256]{2,1,0:T(8,128)(2,1)S(1)} %get-tuple-element.30.vectors, bf16[17,256,128]{2,1,0:T(8,128)(2,1)S(1)} %get-tuple-element.27.near), custom_call_target="tpu_custom_call" | custom-call | flops 805306368 | bytes 5833728 | tf_op jit(solution)/shard_map/pallas_call | solution.py:186
  36.0 0.0 copy-start.8
  36.0 0.0 copy-start.9
  36.0 0.0 collective-permute-done.2.refs_0_
  36.0 0.3 collective-permute-done.3.refs_1_
  36.3 0.0 collective-permute-done.4.refs_2_
  36.3 0.0 copy-done
  36.3 0.0 copy-done.1
  36.3 0.0 copy-done.4
  36.4 0.0 copy-done.7
  36.4 2.2 %shard_map.124 = (f32[384,256]{1,0:T(8,128)S(1)}, f32[64,256]{1,0:T(8,128)S(1)}) custom-call(bf16[4,64,256]{2,1,0:T(8,128)(2,1)S(1)} %shard_map.123.own, bf16[4,64,256]{2,1,0:T(8,128)(2,1)S(1)} %collective-permute-done.2.refs_0_, bf16[4,64,256]{2,1,0:T(8,128)(2,1)S(1)} %collective-permute-done.3.refs_1_, ...), custom_call_target="tpu_custom_call" | custom-call | bytes 1040128 | tf_op jit(solution)/shard_map/pallas_call | solution.py:367
  38.6 1.9 %collective-permute-start.7 = (f32[64,256]{1,0:T(8,128)S(1)}, f32[64,256]{1,0:T(8,128)S(1)}, u32[]{:S(2)}, u32[]{:S(2)}) collective-permute-start(f32[64,256]{1,0:T(8,128)S(1)} %get-tuple-element.35.own), channel_id=1, source_target_pairs={{0,3},{1,2},{2,1},{3,0},{4,7},{5,6},{6,5},{7,4},{8,11},{9,10},{10,... | collective-permute-start | bytes 196616 | tf_op jit(solution)/shard_map/ppermute | solution.py:413
  40.5 1.3 %collective-permute-start.6 = (f32[64,256]{1,0:T(8,128)S(1)}, f32[64,256]{1,0:T(8,128)S(1)}, u32[]{:S(2)}, u32[]{:S(2)}) collective-permute-start(f32[64,256]{1,0:T(8,128)S(1)} %get-tuple-element.35.own), channel_id=1, source_target_pairs={{0,2},{1,3},{2,0},{3,1},{4,6},{5,7},{6,4},{7,5},{8,10},{9,11},{10,... | collective-permute-start | bytes 196616 | tf_op jit(solution)/shard_map/ppermute | solution.py:413
  41.8 0.4 collective-permute-start.5
  42.2 2.3 %collective-permute-done.7.refs_2_ = f32[64,256]{1,0:T(8,128)S(1)} collective-permute-done((f32[64,256]{1,0:T(8,128)S(1)}, f32[64,256]{1,0:T(8,128)S(1)}, u32[]{:S(2)}, u32[]{:S(2)}) %collective-permute-start.7) | collective-permute-done | bytes 65568 | tf_op jit(solution)/shard_map/ppermute | solution.py:413
  44.4 0.5 collective-permute-done.6.refs_1_
  45.0 1.1 %collective-permute-done.5.refs_0_ = f32[64,256]{1,0:T(8,128)S(1)} collective-permute-done((f32[64,256]{1,0:T(8,128)S(1)}, f32[64,256]{1,0:T(8,128)S(1)}, u32[]{:S(2)}, u32[]{:S(2)}) %collective-permute-start.5) | collective-permute-done | bytes 65568 | tf_op jit(solution)/shard_map/ppermute | solution.py:413
  46.1 1.5 %shard_map.125 = (f32[3,64,128]{2,1,0:T(8,128)S(1)}, f32[64,256]{1,0:T(8,128)S(1)}) custom-call(f32[64,256]{1,0:T(8,128)S(1)} %get-tuple-element.35.own, f32[64,256]{1,0:T(8,128)S(1)} %collective-permute-done.5.refs_0_, f32[64,256]{1,0:T(8,128)S(1)} %collective-permute-done.6.refs_1_, f32[64,256]{1,0:T(8,128)S(1)} %collective-permute-done.7.refs_2_, ...), custom_call_target="tpu_custom_call" | custom-call | bytes 511744 | tf_op jit(solution)/shard_map/pallas_call | solution.py:367
  47.5 0.1 collective-permute-start.11
  47.6 1.5 %collective-permute-start.10 = (f32[384,256]{1,0:T(8,128)S(1)}, f32[384,256]{1,0:T(8,128)S(1)}, u32[]{:S(2)}, u32[]{:S(2)}) collective-permute-start(f32[384,256]{1,0:T(8,128)S(1)} %get-tuple-element.37.own), channel_id=1, source_target_pairs={{0,3},{1,2},{2,1},{3,0},{4,7},{5,6},{6,5},{7,4},{8,11},{9,10},{10,... | collective-permute-start | bytes 1179656 | tf_op jit(solution)/shard_map/ppermute | solution.py:413
  49.2 0.3 collective-permute-start.9
  49.5 1.7 %collective-permute-start.8 = (f32[384,256]{1,0:T(8,128)S(1)}, f32[384,256]{1,0:T(8,128)S(1)}, u32[]{:S(2)}, u32[]{:S(2)}) collective-permute-start(f32[384,256]{1,0:T(8,128)S(1)} %get-tuple-element.37.own), channel_id=1, source_target_pairs={{0,1},{1,0},{2,3},{3,2},{4,5},{5,4},{6,7},{7,6},{8,9},{9,8},{10,11... | collective-permute-start | bytes 1179656 | tf_op jit(solution)/shard_map/ppermute | solution.py:413
  51.2 0.0 collective-permute-done.11.arrived
  51.2 0.0 copy-done.8
  51.2 0.0 copy-done.9
  51.2 0.6 shard_map.127
  51.8 3.4 %collective-permute-start.12 = (f32[64,256]{1,0:T(8,128)S(1)}, f32[64,256]{1,0:T(8,128)S(1)}, u32[]{:S(2)}, u32[]{:S(2)}) collective-permute-start(f32[64,256]{1,0:T(8,128)S(1)} %get-tuple-element.42.own), channel_id=1, source_target_pairs={{0,8},{4,12},{8,0},{12,4},{16,24},{20,28},{24,16},{28,20},{1,9},{5... | collective-permute-start | bytes 196616 | tf_op jit(solution)/shard_map/ppermute | solution.py:475
  55.2 2.2 %collective-permute-done.12.arrived = f32[64,256]{1,0:T(8,128)S(1)} collective-permute-done((f32[64,256]{1,0:T(8,128)S(1)}, f32[64,256]{1,0:T(8,128)S(1)}, u32[]{:S(2)}, u32[]{:S(2)}) %collective-permute-start.12) | collective-permute-done | bytes 65568 | tf_op jit(solution)/shard_map/ppermute | solution.py:475
  57.4 0.6 shard_map.128
  58.0 2.7 %collective-permute-start.13 = (f32[64,256]{1,0:T(8,128)S(1)}, f32[64,256]{1,0:T(8,128)S(1)}, u32[]{:S(2)}, u32[]{:S(2)}) collective-permute-start(f32[64,256]{1,0:T(8,128)S(1)} %get-tuple-element.43.own), channel_id=1, source_target_pairs={{0,16},{4,20},{8,24},{12,28},{16,0},{20,4},{24,8},{28,12},{1,17},{... | collective-permute-start | bytes 196616 | tf_op jit(solution)/shard_map/ppermute | solution.py:475
  60.7 2.8 %collective-permute-done.13.arrived = f32[64,256]{1,0:T(8,128)S(1)} collective-permute-done((f32[64,256]{1,0:T(8,128)S(1)}, f32[64,256]{1,0:T(8,128)S(1)}, u32[]{:S(2)}, u32[]{:S(2)}) %collective-permute-start.13) | collective-permute-done | bytes 65568 | tf_op jit(solution)/shard_map/ppermute | solution.py:475
  63.5 1.3 %shard_map.129 = (f32[3,64,128]{2,1,0:T(8,128)}, f32[64,64]{1,0:T(8,128)}) custom-call(f32[64,256]{1,0:T(8,128)S(1)} %get-tuple-element.43.own, f32[64,256]{1,0:T(8,128)S(1)} %collective-permute-done.13.arrived, s32[7,64]{1,0:T(8,128)S(1)} %copy-done.9, f32[7,64,64]{2,1,0:T(8,128)S(1)} %copy-done.8, f32[64,128]{1,0:T(8,128)S(1)} %get-tuple-element.44.refs_0_, ...), custom_call_target="tpu_custom_call" | custom-call | flops 850000000 | bytes 313088 | tf_op jit(solution)/shard_map/pallas_call | solution.py:367
  64.8 0.0 collective-permute-done.10.refs_2_
  64.8 3.6 %collective-permute-done.9.refs_1_ = f32[384,256]{1,0:T(8,128)S(1)} collective-permute-done((f32[384,256]{1,0:T(8,128)S(1)}, f32[384,256]{1,0:T(8,128)S(1)}, u32[]{:S(2)}, u32[]{:S(2)}) %collective-permute-start.9) | collective-permute-done | bytes 393248 | tf_op jit(solution)/shard_map/ppermute | solution.py:413
  68.5 0.0 collective-permute-done.8.refs_0_
  68.5 1.2 %shard_map.126 = (f32[16,64,256]{2,1,0:T(8,128)}, f32[15,64,128]{2,1,0:T(8,128)}) custom-call(f32[384,256]{1,0:T(8,128)S(1)} %get-tuple-element.37.own, f32[384,256]{1,0:T(8,128)S(1)} %collective-permute-done.8.refs_0_, f32[384,256]{1,0:T(8,128)S(1)} %collective-permute-done.9.refs_1_, f32[384,256]{1,0:T(8,128)S(1)} %collective-permute-done.10.refs_2_, ...), custom_call_target="tpu_custom_call" | custom-call | bytes 1671168 | tf_op jit(solution)/shard_map/pallas_call | solution.py:367
  (1 shorter events, 0.0 us)
Async XLA Ops:
  1.4 1.0 %copy-start.2 = (bf16[16,64,256]{2,1,0:T(8,128)(2,1)S(1)}, bf16[16,64,256]{2,1,0:T(8,128)(2,1)}, u32[]{:S(2)}) copy-start(bf16[16,64,256]{2,1,0:T(8,128)(2,1)} %probe.5) | copy-start | bytes 1572868
  2.4 16.5 %copy-start.6 = (s32[16,16]{1,0:T(8,128)S(1)}, s32[16,16]{1,0:T(8,128)}, u32[]{:S(2)}) copy-start(s32[16,16]{1,0:T(8,128)} %nb_ref.5) | copy-start | bytes 3076
  2.5 16.5 %copy-start.3 = (bf16[16,64,256]{2,1,0:T(8,128)(2,1)S(1)}, bf16[16,64,256]{2,1,0:T(8,128)(2,1)}, u32[]{:S(2)}) copy-start(bf16[16,64,256]{2,1,0:T(8,128)(2,1)} %probe.5) | copy-start | bytes 1572868
  2.5 16.5 %collective-permute-start.1 = (bf16[16,80,256]{2,1,0:T(8,128)(2,1)S(1)}, bf16[16,80,256]{2,1,0:T(8,128)(2,1)S(1)}, u32[]{:S(2)}, u32[]{:S(2)}) collective-permute-start(bf16[16,80,256]{2,1,0:T(8,128)(2,1)S(1)} %shard_map.120), channel_id=1, source_target_pairs={{4,0},{8,4},{12,8},{16,12},{20,16},{24,20},{28,24},{5,1},{9,5},{13... | collective-permute-start | bytes 1966088 | tf_op jit(solution)/shard_map/ppermute | solution.py:410
  3.9 15.0 %collective-permute-start = (bf16[16,80,256]{2,1,0:T(8,128)(2,1)S(1)}, bf16[16,80,256]{2,1,0:T(8,128)(2,1)S(1)}, u32[]{:S(2)}, u32[]{:S(2)}) collective-permute-start(bf16[16,80,256]{2,1,0:T(8,128)(2,1)S(1)} %shard_map.120), channel_id=1, source_target_pairs={{0,4},{4,8},{8,12},{12,16},{16,20},{20,24},{24,28},{1,5},{5,9},{9,... | collective-permute-start | bytes 1966088 | tf_op jit(solution)/shard_map/ppermute | solution.py:410
  7.0 0.7 %copy-start.5 = (s32[16,16]{1,0:T(8,128)S(1)}, s32[16,16]{1,0:T(8,128)}, u32[]{:S(2)}) copy-start(s32[16,16]{1,0:T(8,128)} %nb_ref.5) | copy-start | bytes 3076
  26.3 9.7 %collective-permute-start.2 = (bf16[4,64,256]{2,1,0:T(8,128)(2,1)S(1)}, bf16[4,64,256]{2,1,0:T(8,128)(2,1)S(1)}, u32[]{:S(2)}, u32[]{:S(2)}) collective-permute-start(bf16[4,64,256]{2,1,0:T(8,128)(2,1)S(1)} %get-tuple-element.31), channel_id=1, source_target_pairs={{0,1},{1,0},{2,3},{3,2},{4,5},{5,4},{6,7},{7,6},{8,9},{9,8},{10,11... | collective-permute-start | bytes 393224 | tf_op jit(solution)/shard_map/ppermute | solution.py:413
  28.6 7.8 %collective-permute-start.3 = (bf16[4,64,256]{2,1,0:T(8,128)(2,1)S(1)}, bf16[4,64,256]{2,1,0:T(8,128)(2,1)S(1)}, u32[]{:S(2)}, u32[]{:S(2)}) collective-permute-start(bf16[4,64,256]{2,1,0:T(8,128)(2,1)S(1)} %get-tuple-element.32), channel_id=1, source_target_pairs={{0,2},{1,3},{2,0},{3,1},{4,6},{5,7},{6,4},{7,5},{8,10},{9,11},{10,... | collective-permute-start | bytes 393224 | tf_op jit(solution)/shard_map/ppermute | solution.py:413
  29.3 7.0 %collective-permute-start.4 = (bf16[4,64,256]{2,1,0:T(8,128)(2,1)S(1)}, bf16[4,64,256]{2,1,0:T(8,128)(2,1)S(1)}, u32[]{:S(2)}, u32[]{:S(2)}) collective-permute-start(bf16[4,64,256]{2,1,0:T(8,128)(2,1)S(1)} %get-tuple-element.33), channel_id=1, source_target_pairs={{0,3},{1,2},{2,1},{3,0},{4,7},{5,6},{6,5},{7,4},{8,11},{9,10},{10,... | collective-permute-start | bytes 393224 | tf_op jit(solution)/shard_map/ppermute | solution.py:413
  30.1 6.2 %copy-start = (f32[15,64,64]{2,1,0:T(8,128)S(1)}, f32[15,64,64]{2,1,0:T(8,128)}, u32[]{:S(2)}) copy-start(f32[15,64,64]{2,1,0:T(8,128)} %refs_4_.3) | copy-start | bytes 737284
  30.1 6.2 %copy-start.1 = (f32[16,64,64]{2,1,0:T(8,128)S(1)}, f32[16,64,64]{2,1,0:T(8,128)}, u32[]{:S(2)}) copy-start(f32[16,64,64]{2,1,0:T(8,128)} %refs_4_.2) | copy-start | bytes 786436
  30.1 6.2 %copy-start.4 = (s32[15,64]{1,0:T(8,128)S(1)}, s32[15,64]{1,0:T(8,128)}, u32[]{:S(2)}) copy-start(s32[15,64]{1,0:T(8,128)} %refs_3_.3) | copy-start | bytes 11524
  30.1 6.3 %copy-start.7 = (s32[16,64]{1,0:T(8,128)S(1)}, s32[16,64]{1,0:T(8,128)}, u32[]{:S(2)}) copy-start(s32[16,64]{1,0:T(8,128)} %refs_3_.2) | copy-start | bytes 12292
  36.0 15.2 %copy-start.8 = (f32[7,64,64]{2,1,0:T(8,128)S(1)}, f32[7,64,64]{2,1,0:T(8,128)}, u32[]{:S(2)}) copy-start(f32[7,64,64]{2,1,0:T(8,128)} %inverse.5) | copy-start | bytes 344068
  36.0 15.2 %copy-start.9 = (s32[7,64]{1,0:T(8,128)S(1)}, s32[7,64]{1,0:T(8,128)}, u32[]{:S(2)}) copy-start(s32[7,64]{1,0:T(8,128)} %pivots.5) | copy-start | bytes 5380
  38.6 5.8 %collective-permute-start.7 = (f32[64,256]{1,0:T(8,128)S(1)}, f32[64,256]{1,0:T(8,128)S(1)}, u32[]{:S(2)}, u32[]{:S(2)}) collective-permute-start(f32[64,256]{1,0:T(8,128)S(1)} %get-tuple-element.35.own), channel_id=1, source_target_pairs={{0,3},{1,2},{2,1},{3,0},{4,7},{5,6},{6,5},{7,4},{8,11},{9,10},{10,... | collective-permute-start | bytes 196616 | tf_op jit(solution)/shard_map/ppermute | solution.py:413
  40.5 4.4 %collective-permute-start.6 = (f32[64,256]{1,0:T(8,128)S(1)}, f32[64,256]{1,0:T(8,128)S(1)}, u32[]{:S(2)}, u32[]{:S(2)}) collective-permute-start(f32[64,256]{1,0:T(8,128)S(1)} %get-tuple-element.35.own), channel_id=1, source_target_pairs={{0,2},{1,3},{2,0},{3,1},{4,6},{5,7},{6,4},{7,5},{8,10},{9,11},{10,... | collective-permute-start | bytes 196616 | tf_op jit(solution)/shard_map/ppermute | solution.py:413
  41.8 4.3 %collective-permute-start.5 = (f32[64,256]{1,0:T(8,128)S(1)}, f32[64,256]{1,0:T(8,128)S(1)}, u32[]{:S(2)}, u32[]{:S(2)}) collective-permute-start(f32[64,256]{1,0:T(8,128)S(1)} %get-tuple-element.35.own), channel_id=1, source_target_pairs={{0,1},{1,0},{2,3},{3,2},{4,5},{5,4},{6,7},{7,6},{8,9},{9,8},{10,11... | collective-permute-start | bytes 196616 | tf_op jit(solution)/shard_map/ppermute | solution.py:413
  47.5 3.6 %collective-permute-start.11 = (f32[64,256]{1,0:T(8,128)S(1)}, f32[64,256]{1,0:T(8,128)S(1)}, u32[]{:S(2)}, u32[]{:S(2)}) collective-permute-start(f32[64,256]{1,0:T(8,128)S(1)} %get-tuple-element.41.own), channel_id=1, source_target_pairs={{0,4},{4,0},{8,12},{12,8},{16,20},{20,16},{24,28},{28,24},{1,5},{5... | collective-permute-start | bytes 196616 | tf_op jit(solution)/shard_map/ppermute | solution.py:475
  47.6 17.2 %collective-permute-start.10 = (f32[384,256]{1,0:T(8,128)S(1)}, f32[384,256]{1,0:T(8,128)S(1)}, u32[]{:S(2)}, u32[]{:S(2)}) collective-permute-start(f32[384,256]{1,0:T(8,128)S(1)} %get-tuple-element.37.own), channel_id=1, source_target_pairs={{0,3},{1,2},{2,1},{3,0},{4,7},{5,6},{6,5},{7,4},{8,11},{9,10},{10,... | collective-permute-start | bytes 1179656 | tf_op jit(solution)/shard_map/ppermute | solution.py:413
  49.2 19.3 %collective-permute-start.9 = (f32[384,256]{1,0:T(8,128)S(1)}, f32[384,256]{1,0:T(8,128)S(1)}, u32[]{:S(2)}, u32[]{:S(2)}) collective-permute-start(f32[384,256]{1,0:T(8,128)S(1)} %get-tuple-element.37.own), channel_id=1, source_target_pairs={{0,2},{1,3},{2,0},{3,1},{4,6},{5,7},{6,4},{7,5},{8,10},{9,11},{10,... | collective-permute-start | bytes 1179656 | tf_op jit(solution)/shard_map/ppermute | solution.py:413
  49.5 19.0 %collective-permute-start.8 = (f32[384,256]{1,0:T(8,128)S(1)}, f32[384,256]{1,0:T(8,128)S(1)}, u32[]{:S(2)}, u32[]{:S(2)}) collective-permute-start(f32[384,256]{1,0:T(8,128)S(1)} %get-tuple-element.37.own), channel_id=1, source_target_pairs={{0,1},{1,0},{2,3},{3,2},{4,5},{5,4},{6,7},{7,6},{8,9},{9,8},{10,11... | collective-permute-start | bytes 1179656 | tf_op jit(solution)/shard_map/ppermute | solution.py:413
  51.8 5.6 %collective-permute-start.12 = (f32[64,256]{1,0:T(8,128)S(1)}, f32[64,256]{1,0:T(8,128)S(1)}, u32[]{:S(2)}, u32[]{:S(2)}) collective-permute-start(f32[64,256]{1,0:T(8,128)S(1)} %get-tuple-element.42.own), channel_id=1, source_target_pairs={{0,8},{4,12},{8,0},{12,4},{16,24},{20,28},{24,16},{28,20},{1,9},{5... | collective-permute-start | bytes 196616 | tf_op jit(solution)/shard_map/ppermute | solution.py:475
  58.0 5.4 %collective-permute-start.13 = (f32[64,256]{1,0:T(8,128)S(1)}, f32[64,256]{1,0:T(8,128)S(1)}, u32[]{:S(2)}, u32[]{:S(2)}) collective-permute-start(f32[64,256]{1,0:T(8,128)S(1)} %get-tuple-element.43.own), channel_id=1, source_target_pairs={{0,16},{4,20},{8,24},{12,28},{16,0},{20,4},{24,8},{28,12},{1,17},{... | collective-permute-start | bytes 196616 | tf_op jit(solution)/shard_map/ppermute | solution.py:475
where the time goes:
time: 71.1 us; the launch traced here: 69.7 us
  Pallas kernels  31.9 us (45%)
  starting transfers between devices  21.5 us (30%)
  waiting for transfers between devices  12.9 us (18%)
  local copies, waits for them, and re-layouts  2.52 us (4%)
  between operations  0.83 us (1%)
    pallas_call x3, Pallas kernels, near_call(): pl.pallas_call(body, out_shape=outs, in_specs=[pl.BlockSpec(memory_space=...  24.4 us
    ppermute x9, starting transfers between devices, vec_send(): return lax.ppermute(array, 'vec', [(i, i ^ tier) for i in range(parts)])  10.9 us
    ppermute x9, waiting for transfers between devices, vec_send(): return lax.ppermute(array, 'vec', [(i, i ^ tier) for i in range(parts)])  7.86 us
    pallas_call x7, Pallas kernels, call(): pl.pallas_call(body, out_shape=outs, in_specs=[pl.BlockSpec(memory_space=...  7.53 us
    ppermute x3, starting transfers between devices, on_device(): lax.ppermute(own_up, 'leaf', [(i, i ^ 1 << tier) for i in range(leaf_tota...  6.11 us
    ppermute x3, waiting for transfers between devices, on_device(): lax.ppermute(own_up, 'leaf', [(i, i ^ 1 << tier) for i in range(leaf_tota...  5.04 us
    ppermute x1, starting transfers between devices, on_device(): lax.ppermute(joined, 'leaf', up)  3.07 us
    unnamed x21, local copies, waits for them, and re-layouts  2.52 us
  transfers between devices with their start and end apart: 14, of which 7 were waited for; matrix products, arithmetic and copies ran while one was open for 0% of the time, Pallas kernels for 28%

commit v1 on v0

--- a/solution.py
+++ b/solution.py
@@ -13,7 +13,8 @@
 EPSILON = 1e-06
 FLIGHT = 8
 DEPTH = 128
-ROUND_FLOPS = 850_000_000
+LATE = (2,)
+ROUND_FLOPS = 400_000_000
 VMEM_BYTES = 20 * 1024 * 1024
 VMEM = pltpu.MemorySpace.VMEM
 SMEM = pltpu.MemorySpace.SMEM
@@ -104,9 +105,7 @@
         position = code % 64
         for top in range(0, size, 128):
             distance = nn(near[row, top : top + 128, :], far[position])
-            tile[top : top + 128, :] = jnp.exp2(-0.5 * jnp.log2(distance)).astype(
-                jnp.bfloat16
-            )
+            tile[top : top + 128, :] = lax.rsqrt(distance).astype(jnp.bfloat16)
 
     def step(index, carry):
         for way in range(flight):
@@ -465,8 +464,9 @@
         [own_up] + near_ups + [local_pivots, local_inverse],
     )
 
-    pack, own_up = lax.optimization_barrier((pack, own_up))
-    others = [vec_send(pack, tier) for tier in range(1, parts)]
+    later, own_up = lax.optimization_barrier((pack, own_up))
+    late = LATE if parts > max(LATE) else ()
+    others = [vec_send(later if tier in late else pack, tier) for tier in range(1, parts)]
 
     heap_first = 0
     maps = []

time: 71.1 us -> 65.6 us (0.923); the launches traced: 69.7 us -> 65.8 us
  Pallas kernels: 31.9 us -> 28.3 us
  waiting for transfers between devices: 12.9 us -> 9.58 us
  starting transfers between devices: 21.5 us -> 24.5 us
    ppermute x9, waiting for transfers between devices: 7.86 us -> 3.05 us  [vec_send(): return lax.ppermute(array, 'vec', [(i, i ^ tier) for i in range(parts)])]
    pallas_call x3, Pallas kernels: 24.4 us -> 20.8 us  [near_call(): pl.pallas_call(body, out_shape=outs, in_specs=[pl.BlockSpec(memory_space=...]
    ppermute x3, starting transfers between devices: 6.11 us -> 8 us  [on_device(): lax.ppermute(own_up, 'leaf', [(i, i ^ 1 << tier) for i in range(leaf_tota...]
    ppermute x3, waiting for transfers between devices: 5.04 us -> 6.53 us  [on_device(): lax.ppermute(own_up, 'leaf', [(i, i ^ 1 << tier) for i in range(leaf_tota...]
    ppermute x9, starting transfers between devices: 10.9 us -> 12 us  [vec_send(): return lax.ppermute(array, 'vec', [(i, i ^ tier) for i in range(parts)])]
  transfers between devices with their start and end apart: 14 -> 14, of which waited for: 7 -> 6; matrix products, arithmetic and copies ran while one was open for 0% -> 0% of each run, Pallas kernels for 28% -> 28%
where the time goes in v1:
time: 65.6 us; the launch traced here: 65.8 us
  Pallas kernels  28.3 us (43%)
  starting transfers between devices  24.5 us (37%)
  waiting for transfers between devices  9.58 us (15%)
  local copies, waits for them, and re-layouts  2.53 us (4%)
  between operations  0.83 us (1%)
    pallas_call x3, Pallas kernels, near_call(): pl.pallas_call(body, out_shape=outs, in_specs=[pl.BlockSpec(memory_space=...  20.8 us
    ppermute x9, starting transfers between devices, vec_send(): return lax.ppermute(array, 'vec', [(i, i ^ tier) for i in range(parts)])  12 us
    ppermute x3, starting transfers between devices, on_device(): lax.ppermute(own_up, 'leaf', [(i, i ^ 1 << tier) for i in range(leaf_tota...  8 us
    pallas_call x7, Pallas kernels, call(): pl.pallas_call(body, out_shape=outs, in_specs=[pl.BlockSpec(memory_space=...  7.53 us
    ppermute x3, waiting for transfers between devices, on_device(): lax.ppermute(own_up, 'leaf', [(i, i ^ 1 << tier) for i in range(leaf_tota...  6.53 us
    ppermute x1, starting transfers between devices, on_device(): lax.ppermute(joined, 'leaf', up)  3.07 us
    ppermute x9, waiting for transfers between devices, vec_send(): return lax.ppermute(array, 'vec', [(i, i ^ tier) for i in range(parts)])  3.05 us
    unnamed x21, local copies, waits for them, and re-layouts  2.53 us
  transfers between devices with their start and end apart: 14, of which 6 were waited for; matrix products, arithmetic and copies ran while one was open for 0% of the time, Pallas kernels for 28%

profile of v1, /device:TPU:0, one launch (start us, length us, event | category | flops | bytes accessed | tf_op | source)
XLA Modules:
  0.0 65.8 jit_solution(11952102050254890705)
XLA Ops:
  0.6 0.8 %copy.13.points = bf16[16,3,256]{2,1,0:T(4,128)(2,1)S(1)} copy(bf16[16,3,256]{2,0,1:T(8,128)(2,1)} %param.9) | data formatting | bytes 49152 | tf_op args[0]
  1.4 0.0 copy-start.2
  1.4 1.0 %copy-done.2 = bf16[16,64,256]{2,1,0:T(8,128)(2,1)S(1)} copy-done((bf16[16,64,256]{2,1,0:T(8,128)(2,1)S(1)}, bf16[16,64,256]{2,1,0:T(8,128)(2,1)}, u32[]{:S(2)}) %copy-start.2) | copy-done | bytes 524312
  2.4 0.0 copy-start.6
  2.5 0.0 copy-start.3
  2.5 1.4 %collective-permute-start.1 = (bf16[16,80,256]{2,1,0:T(8,128)(2,1)S(1)}, bf16[16,80,256]{2,1,0:T(8,128)(2,1)S(1)}, u32[]{:S(2)}, u32[]{:S(2)}) collective-permute-start(bf16[16,80,256]{2,1,0:T(8,128)(2,1)S(1)} %shard_map.120), channel_id=1, source_target_pairs={{4,0},{8,4},{12,8},{16,12},{20,16},{24,20},{28,24},{5,1},{9,5},{13... | collective-permute-start | bytes 1966088 | tf_op jit(solution)/shard_map/ppermute | solution.py:409
  3.9 3.1 %collective-permute-start = (bf16[16,80,256]{2,1,0:T(8,128)(2,1)S(1)}, bf16[16,80,256]{2,1,0:T(8,128)(2,1)S(1)}, u32[]{:S(2)}, u32[]{:S(2)}) collective-permute-start(bf16[16,80,256]{2,1,0:T(8,128)(2,1)S(1)} %shard_map.120), channel_id=1, source_target_pairs={{0,4},{4,8},{8,12},{12,16},{16,20},{20,24},{24,28},{1,5},{5,9},{9,... | collective-permute-start | bytes 1966088 | tf_op jit(solution)/shard_map/ppermute | solution.py:409
  7.0 0.0 copy-start.5
  7.0 0.7 %copy-done.5 = s32[16,16]{1,0:T(8,128)S(1)} copy-done((s32[16,16]{1,0:T(8,128)S(1)}, s32[16,16]{1,0:T(8,128)}, u32[]{:S(2)}) %copy-start.5) | copy-done | bytes 1048
  7.7 9.8 %shard_map.121 = (f32[17,64,256]{2,1,0:T(8,128)S(1)}, bf16[16,128,256]{2,1,0:T(8,128)(2,1)S(1)}, bf16[17,256,128]{2,1,0:T(8,128)(2,1)S(1)}) custom-call(s32[16,16]{1,0:T(8,128)S(1)} %copy-done.5, bf16[16,3,256]{2,1,0:T(4,128)(2,1)S(1)} %copy.13.points, bf16[16,64,256]{2,1,0:T(8,128)(2,1)S(1)} %copy-done.2), custom_call_target="tpu_custom_call" | custom-call | flops 1207959552 | bytes 549888 | tf_op jit(solution)/shard_map/pallas_call | solution.py:185
  17.5 0.0 collective-permute-done.1.after
  17.5 0.0 collective-permute-done.before
  17.5 0.0 copy-done.6
  17.5 0.0 copy-done.3
  17.6 6.2 %shard_map.122 = (bf16[4,64,256]{2,1,0:T(8,128)(2,1)S(1)}, bf16[4,64,256]{2,1,0:T(8,128)(2,1)S(1)}, bf16[4,64,256]{2,1,0:T(8,128)(2,1)S(1)}, bf16[48,128,256]{2,1,0:T(8,128)(2,1)S(1)}, bf16[48,64,256]{2,1,0:T(8,128)(2,1)S(1)}) custom-call(s32[16,16]{1,0:T(8,128)S(1)} %copy-done.6, bf16[16,64,256]{2,1,0:T(8,128)(2,1)S(1)} %copy-done.3, ...), custom_call_target="tpu_custom_call" | custom-call | flops 1207959552 | bytes 5112832 | tf_op jit(solution)/shard_map/pallas_call | solution.py:185
  23.7 2.3 %collective-permute-start.2 = (bf16[4,64,256]{2,1,0:T(8,128)(2,1)S(1)}, bf16[4,64,256]{2,1,0:T(8,128)(2,1)S(1)}, u32[]{:S(2)}, u32[]{:S(2)}) collective-permute-start(bf16[4,64,256]{2,1,0:T(8,128)(2,1)S(1)} %get-tuple-element.31), channel_id=1, source_target_pairs={{0,1},{1,0},{2,3},{3,2},{4,5},{5,4},{6,7},{7,6},{8,9},{9,8},{10,11... | collective-permute-start | bytes 393224 | tf_op jit(solution)/shard_map/ppermute | solution.py:412
  26.1 2.2 %collective-permute-start.3 = (bf16[4,64,256]{2,1,0:T(8,128)(2,1)S(1)}, bf16[4,64,256]{2,1,0:T(8,128)(2,1)S(1)}, u32[]{:S(2)}, u32[]{:S(2)}) collective-permute-start(bf16[4,64,256]{2,1,0:T(8,128)(2,1)S(1)} %get-tuple-element.32), channel_id=1, source_target_pairs={{0,2},{1,3},{2,0},{3,1},{4,6},{5,7},{6,4},{7,5},{8,10},{9,11},{10,... | collective-permute-start | bytes 393224 | tf_op jit(solution)/shard_map/ppermute | solution.py:412
  28.3 0.0 collective-permute-start.4
  28.3 0.0 copy-start
  28.3 0.0 copy-start.1
  28.3 0.0 copy-start.4
  28.3 0.0 copy-start.7
  28.3 4.8 %shard_map.123.own = bf16[4,64,256]{2,1,0:T(8,128)(2,1)S(1)} custom-call(s32[16,16]{1,0:T(8,128)S(1)} %copy-done.6, bf16[48,128,256]{2,1,0:T(8,128)(2,1)S(1)} %get-tuple-element.29.far, bf16[48,64,256]{2,1,0:T(8,128)(2,1)S(1)} %get-tuple-element.30.vectors, bf16[17,256,128]{2,1,0:T(8,128)(2,1)S(1)} %get-tuple-element.27.near), custom_call_target="tpu_custom_call" | custom-call | flops 805306368 | bytes 5833728 | tf_op jit(solution)/shard_map/pallas_call | solution.py:185
  33.1 0.0 copy-start.8
  33.1 0.0 copy-start.9
  33.1 0.0 collective-permute-done.2.refs_0_
  33.1 1.8 %collective-permute-done.3.refs_1_ = bf16[4,64,256]{2,1,0:T(8,128)(2,1)S(1)} collective-permute-done((bf16[4,64,256]{2,1,0:T(8,128)(2,1)S(1)}, bf16[4,64,256]{2,1,0:T(8,128)(2,1)S(1)}, u32[]{:S(2)}, u32[]{:S(2)}) %collective-permute-start.3) | collective-permute-done | bytes 131104 | tf_op jit(solution)/shard_map/ppermute | solution.py:412
  34.9 0.0 collective-permute-done.4.refs_2_
  34.9 0.0 copy-done
  34.9 0.0 copy-done.1
  34.9 0.0 copy-done.4
  34.9 0.0 copy-done.7
  35.0 2.2 %shard_map.124 = (f32[384,256]{1,0:T(8,128)S(1)}, f32[64,256]{1,0:T(8,128)S(1)}) custom-call(bf16[4,64,256]{2,1,0:T(8,128)(2,1)S(1)} %shard_map.123.own, bf16[4,64,256]{2,1,0:T(8,128)(2,1)S(1)} %collective-permute-done.2.refs_0_, bf16[4,64,256]{2,1,0:T(8,128)(2,1)S(1)} %collective-permute-done.3.refs_1_, ...), custom_call_target="tpu_custom_call" | custom-call | bytes 1040128 | tf_op jit(solution)/shard_map/pallas_call | solution.py:366
  37.2 1.6 %collective-permute-start.8 = (f32[64,256]{1,0:T(8,128)S(1)}, f32[64,256]{1,0:T(8,128)S(1)}, u32[]{:S(2)}, u32[]{:S(2)}) collective-permute-start(f32[64,256]{1,0:T(8,128)S(1)} %get-tuple-element.35.own), channel_id=1, source_target_pairs={{0,3},{1,2},{2,1},{3,0},{4,7},{5,6},{6,5},{7,4},{8,11},{9,10},{10,... | collective-permute-start | bytes 196616 | tf_op jit(solution)/shard_map/ppermute | solution.py:412
  38.8 1.4 %collective-permute-start.7 = (f32[64,256]{1,0:T(8,128)S(1)}, f32[64,256]{1,0:T(8,128)S(1)}, u32[]{:S(2)}, u32[]{:S(2)}) collective-permute-start(f32[64,256]{1,0:T(8,128)S(1)} %get-tuple-element.35.own), channel_id=1, source_target_pairs={{0,2},{1,3},{2,0},{3,1},{4,6},{5,7},{6,4},{7,5},{8,10},{9,11},{10,... | collective-permute-start | bytes 196616 | tf_op jit(solution)/shard_map/ppermute | solution.py:412
  40.2 0.6 collective-permute-start.6
  40.8 1.5 %collective-permute-start.10 = (f32[384,256]{1,0:T(8,128)S(1)}, f32[384,256]{1,0:T(8,128)S(1)}, u32[]{:S(2)}, u32[]{:S(2)}) collective-permute-start(f32[384,256]{1,0:T(8,128)S(1)} %get-tuple-element.37.own), channel_id=1, source_target_pairs={{0,3},{1,2},{2,1},{3,0},{4,7},{5,6},{6,5},{7,4},{8,11},{9,10},{10,... | collective-permute-start | bytes 1179656 | tf_op jit(solution)/shard_map/ppermute | solution.py:412
  42.3 1.7 %collective-permute-start.5 = (f32[384,256]{1,0:T(8,128)S(1)}, f32[384,256]{1,0:T(8,128)S(1)}, u32[]{:S(2)}, u32[]{:S(2)}) collective-permute-start(f32[384,256]{1,0:T(8,128)S(1)} %get-tuple-element.37.own), channel_id=1, source_target_pairs={{0,1},{1,0},{2,3},{3,2},{4,5},{5,4},{6,7},{7,6},{8,9},{9,8},{10,11... | collective-permute-start | bytes 1179656 | tf_op jit(solution)/shard_map/ppermute | solution.py:412
  44.0 0.0 collective-permute-done.8.refs_2_
  44.0 0.3 collective-permute-done.7.refs_1_
  44.3 0.9 %collective-permute-done.6.refs_0_ = f32[64,256]{1,0:T(8,128)S(1)} collective-permute-done((f32[64,256]{1,0:T(8,128)S(1)}, f32[64,256]{1,0:T(8,128)S(1)}, u32[]{:S(2)}, u32[]{:S(2)}) %collective-permute-start.6) | collective-permute-done | bytes 65568 | tf_op jit(solution)/shard_map/ppermute | solution.py:412
  45.2 1.5 %shard_map.125 = (f32[3,64,128]{2,1,0:T(8,128)S(1)}, f32[64,256]{1,0:T(8,128)S(1)}) custom-call(f32[64,256]{1,0:T(8,128)S(1)} %get-tuple-element.35.own, f32[64,256]{1,0:T(8,128)S(1)} %collective-permute-done.6.refs_0_, f32[64,256]{1,0:T(8,128)S(1)} %collective-permute-done.7.refs_1_, f32[64,256]{1,0:T(8,128)S(1)} %collective-permute-done.8.refs_2_, ...), custom_call_target="tpu_custom_call" | custom-call | bytes 511744 | tf_op jit(solution)/shard_map/pallas_call | solution.py:366
  46.7 0.7 %collective-permute-start.9 = (f32[384,256]{1,0:T(8,128)S(1)}, f32[384,256]{1,0:T(8,128)S(1)}, u32[]{:S(2)}, u32[]{:S(2)}) collective-permute-start(f32[384,256]{1,0:T(8,128)S(1)} %get-tuple-element.37.own), channel_id=1, source_target_pairs={{0,2},{1,3},{2,0},{3,1},{4,6},{5,7},{6,4},{7,5},{8,10},{9,11},{10,... | collective-permute-start | bytes 1179656 | tf_op jit(solution)/shard_map/ppermute | solution.py:412
  47.4 0.0 collective-permute-start.11
  47.4 1.3 %collective-permute-done.11.arrived = f32[64,256]{1,0:T(8,128)S(1)} collective-permute-done((f32[64,256]{1,0:T(8,128)S(1)}, f32[64,256]{1,0:T(8,128)S(1)}, u32[]{:S(2)}, u32[]{:S(2)}) %collective-permute-start.11) | collective-permute-done | bytes 65568 | tf_op jit(solution)/shard_map/ppermute | solution.py:475
  48.7 0.0 copy-done.8
  48.7 0.0 copy-done.9
  48.7 0.6 shard_map.127
  49.3 1.9 %collective-permute-start.12 = (f32[64,256]{1,0:T(8,128)S(1)}, f32[64,256]{1,0:T(8,128)S(1)}, u32[]{:S(2)}, u32[]{:S(2)}) collective-permute-start(f32[64,256]{1,0:T(8,128)S(1)} %get-tuple-element.42.own), channel_id=1, source_target_pairs={{0,8},{4,12},{8,0},{12,4},{16,24},{20,28},{24,16},{28,20},{1,9},{5... | collective-permute-start | bytes 196616 | tf_op jit(solution)/shard_map/ppermute | solution.py:475
  51.2 2.4 %collective-permute-done.12.arrived = f32[64,256]{1,0:T(8,128)S(1)} collective-permute-done((f32[64,256]{1,0:T(8,128)S(1)}, f32[64,256]{1,0:T(8,128)S(1)}, u32[]{:S(2)}, u32[]{:S(2)}) %collective-permute-start.12) | collective-permute-done | bytes 65568 | tf_op jit(solution)/shard_map/ppermute | solution.py:475
  53.6 0.6 shard_map.128
  54.2 6.1 %collective-permute-start.13 = (f32[64,256]{1,0:T(8,128)S(1)}, f32[64,256]{1,0:T(8,128)S(1)}, u32[]{:S(2)}, u32[]{:S(2)}) collective-permute-start(f32[64,256]{1,0:T(8,128)S(1)} %get-tuple-element.43.own), channel_id=1, source_target_pairs={{0,16},{4,20},{8,24},{12,28},{16,0},{20,4},{24,8},{28,12},{1,17},{... | collective-permute-start | bytes 196616 | tf_op jit(solution)/shard_map/ppermute | solution.py:475
  60.3 2.9 %collective-permute-done.13.arrived = f32[64,256]{1,0:T(8,128)S(1)} collective-permute-done((f32[64,256]{1,0:T(8,128)S(1)}, f32[64,256]{1,0:T(8,128)S(1)}, u32[]{:S(2)}, u32[]{:S(2)}) %collective-permute-start.13) | collective-permute-done | bytes 65568 | tf_op jit(solution)/shard_map/ppermute | solution.py:475
  63.2 1.3 %shard_map.129 = (f32[3,64,128]{2,1,0:T(8,128)}, f32[64,64]{1,0:T(8,128)}) custom-call(f32[64,256]{1,0:T(8,128)S(1)} %get-tuple-element.43.own, f32[64,256]{1,0:T(8,128)S(1)} %collective-permute-done.13.arrived, s32[7,64]{1,0:T(8,128)S(1)} %copy-done.9, f32[7,64,64]{2,1,0:T(8,128)S(1)} %copy-done.8, f32[64,128]{1,0:T(8,128)S(1)} %get-tuple-element.44.refs_0_, ...), custom_call_target="tpu_custom_call" | custom-call | flops 400000000 | bytes 313088 | tf_op jit(solution)/shard_map/pallas_call | solution.py:366
  64.5 0.0 collective-permute-done.10.refs_2_
  64.5 0.0 collective-permute-done.5.refs_0_
  64.5 0.0 collective-permute-done.9.refs_1_
  64.5 1.2 %shard_map.126 = (f32[16,64,256]{2,1,0:T(8,128)}, f32[15,64,128]{2,1,0:T(8,128)}) custom-call(f32[384,256]{1,0:T(8,128)S(1)} %get-tuple-element.37.own, f32[384,256]{1,0:T(8,128)S(1)} %collective-permute-done.5.refs_0_, f32[384,256]{1,0:T(8,128)S(1)} %collective-permute-done.9.refs_1_, f32[384,256]{1,0:T(8,128)S(1)} %collective-permute-done.10.refs_2_, ...), custom_call_target="tpu_custom_call" | custom-call | bytes 1671168 | tf_op jit(solution)/shard_map/pallas_call | solution.py:366
  (1 shorter events, 0.0 us)
Async XLA Ops:
  1.4 1.0 %copy-start.2 = (bf16[16,64,256]{2,1,0:T(8,128)(2,1)S(1)}, bf16[16,64,256]{2,1,0:T(8,128)(2,1)}, u32[]{:S(2)}) copy-start(bf16[16,64,256]{2,1,0:T(8,128)(2,1)} %probe.5) | copy-start | bytes 1572868
  2.4 15.1 %copy-start.6 = (s32[16,16]{1,0:T(8,128)S(1)}, s32[16,16]{1,0:T(8,128)}, u32[]{:S(2)}) copy-start(s32[16,16]{1,0:T(8,128)} %nb_ref.5) | copy-start | bytes 3076
  2.5 15.1 %copy-start.3 = (bf16[16,64,256]{2,1,0:T(8,128)(2,1)S(1)}, bf16[16,64,256]{2,1,0:T(8,128)(2,1)}, u32[]{:S(2)}) copy-start(bf16[16,64,256]{2,1,0:T(8,128)(2,1)} %probe.5) | copy-start | bytes 1572868
  2.5 15.0 %collective-permute-start.1 = (bf16[16,80,256]{2,1,0:T(8,128)(2,1)S(1)}, bf16[16,80,256]{2,1,0:T(8,128)(2,1)S(1)}, u32[]{:S(2)}, u32[]{:S(2)}) collective-permute-start(bf16[16,80,256]{2,1,0:T(8,128)(2,1)S(1)} %shard_map.120), channel_id=1, source_target_pairs={{4,0},{8,4},{12,8},{16,12},{20,16},{24,20},{28,24},{5,1},{9,5},{13... | collective-permute-start | bytes 1966088 | tf_op jit(solution)/shard_map/ppermute | solution.py:409
  3.9 13.6 %collective-permute-start = (bf16[16,80,256]{2,1,0:T(8,128)(2,1)S(1)}, bf16[16,80,256]{2,1,0:T(8,128)(2,1)S(1)}, u32[]{:S(2)}, u32[]{:S(2)}) collective-permute-start(bf16[16,80,256]{2,1,0:T(8,128)(2,1)S(1)} %shard_map.120), channel_id=1, source_target_pairs={{0,4},{4,8},{8,12},{12,16},{16,20},{20,24},{24,28},{1,5},{5,9},{9,... | collective-permute-start | bytes 1966088 | tf_op jit(solution)/shard_map/ppermute | solution.py:409
  7.0 0.7 %copy-start.5 = (s32[16,16]{1,0:T(8,128)S(1)}, s32[16,16]{1,0:T(8,128)}, u32[]{:S(2)}) copy-start(s32[16,16]{1,0:T(8,128)} %nb_ref.5) | copy-start | bytes 3076
  23.7 9.4 %collective-permute-start.2 = (bf16[4,64,256]{2,1,0:T(8,128)(2,1)S(1)}, bf16[4,64,256]{2,1,0:T(8,128)(2,1)S(1)}, u32[]{:S(2)}, u32[]{:S(2)}) collective-permute-start(bf16[4,64,256]{2,1,0:T(8,128)(2,1)S(1)} %get-tuple-element.31), channel_id=1, source_target_pairs={{0,1},{1,0},{2,3},{3,2},{4,5},{5,4},{6,7},{7,6},{8,9},{9,8},{10,11... | collective-permute-start | bytes 393224 | tf_op jit(solution)/shard_map/ppermute | solution.py:412
  26.1 8.9 %collective-permute-start.3 = (bf16[4,64,256]{2,1,0:T(8,128)(2,1)S(1)}, bf16[4,64,256]{2,1,0:T(8,128)(2,1)S(1)}, u32[]{:S(2)}, u32[]{:S(2)}) collective-permute-start(bf16[4,64,256]{2,1,0:T(8,128)(2,1)S(1)} %get-tuple-element.32), channel_id=1, source_target_pairs={{0,2},{1,3},{2,0},{3,1},{4,6},{5,7},{6,4},{7,5},{8,10},{9,11},{10,... | collective-permute-start | bytes 393224 | tf_op jit(solution)/shard_map/ppermute | solution.py:412
  28.3 6.7 %collective-permute-start.4 = (bf16[4,64,256]{2,1,0:T(8,128)(2,1)S(1)}, bf16[4,64,256]{2,1,0:T(8,128)(2,1)S(1)}, u32[]{:S(2)}, u32[]{:S(2)}) collective-permute-start(bf16[4,64,256]{2,1,0:T(8,128)(2,1)S(1)} %get-tuple-element.33), channel_id=1, source_target_pairs={{0,3},{1,2},{2,1},{3,0},{4,7},{5,6},{6,5},{7,4},{8,11},{9,10},{10,... | collective-permute-start | bytes 393224 | tf_op jit(solution)/shard_map/ppermute | solution.py:412
  28.3 6.7 %copy-start = (f32[15,64,64]{2,1,0:T(8,128)S(1)}, f32[15,64,64]{2,1,0:T(8,128)}, u32[]{:S(2)}) copy-start(f32[15,64,64]{2,1,0:T(8,128)} %refs_4_.3) | copy-start | bytes 737284
  28.3 6.7 %copy-start.1 = (f32[16,64,64]{2,1,0:T(8,128)S(1)}, f32[16,64,64]{2,1,0:T(8,128)}, u32[]{:S(2)}) copy-start(f32[16,64,64]{2,1,0:T(8,128)} %refs_4_.2) | copy-start | bytes 786436
  28.3 6.7 %copy-start.4 = (s32[15,64]{1,0:T(8,128)S(1)}, s32[15,64]{1,0:T(8,128)}, u32[]{:S(2)}) copy-start(s32[15,64]{1,0:T(8,128)} %refs_3_.3) | copy-start | bytes 11524
  28.3 6.7 %copy-start.7 = (s32[16,64]{1,0:T(8,128)S(1)}, s32[16,64]{1,0:T(8,128)}, u32[]{:S(2)}) copy-start(s32[16,64]{1,0:T(8,128)} %refs_3_.2) | copy-start | bytes 12292
  33.1 15.6 %copy-start.8 = (f32[7,64,64]{2,1,0:T(8,128)S(1)}, f32[7,64,64]{2,1,0:T(8,128)}, u32[]{:S(2)}) copy-start(f32[7,64,64]{2,1,0:T(8,128)} %inverse.5) | copy-start | bytes 344068
  33.1 15.6 %copy-start.9 = (s32[7,64]{1,0:T(8,128)S(1)}, s32[7,64]{1,0:T(8,128)}, u32[]{:S(2)}) copy-start(s32[7,64]{1,0:T(8,128)} %pivots.5) | copy-start | bytes 5380
  37.2 6.8 %collective-permute-start.8 = (f32[64,256]{1,0:T(8,128)S(1)}, f32[64,256]{1,0:T(8,128)S(1)}, u32[]{:S(2)}, u32[]{:S(2)}) collective-permute-start(f32[64,256]{1,0:T(8,128)S(1)} %get-tuple-element.35.own), channel_id=1, source_target_pairs={{0,3},{1,2},{2,1},{3,0},{4,7},{5,6},{6,5},{7,4},{8,11},{9,10},{10,... | collective-permute-start | bytes 196616 | tf_op jit(solution)/shard_map/ppermute | solution.py:412
  38.8 5.5 %collective-permute-start.7 = (f32[64,256]{1,0:T(8,128)S(1)}, f32[64,256]{1,0:T(8,128)S(1)}, u32[]{:S(2)}, u32[]{:S(2)}) collective-permute-start(f32[64,256]{1,0:T(8,128)S(1)} %get-tuple-element.35.own), channel_id=1, source_target_pairs={{0,2},{1,3},{2,0},{3,1},{4,6},{5,7},{6,4},{7,5},{8,10},{9,11},{10,... | collective-permute-start | bytes 196616 | tf_op jit(solution)/shard_map/ppermute | solution.py:412
  40.2 5.0 %collective-permute-start.6 = (f32[64,256]{1,0:T(8,128)S(1)}, f32[64,256]{1,0:T(8,128)S(1)}, u32[]{:S(2)}, u32[]{:S(2)}) collective-permute-start(f32[64,256]{1,0:T(8,128)S(1)} %get-tuple-element.35.own), channel_id=1, source_target_pairs={{0,1},{1,0},{2,3},{3,2},{4,5},{5,4},{6,7},{7,6},{8,9},{9,8},{10,11... | collective-permute-start | bytes 196616 | tf_op jit(solution)/shard_map/ppermute | solution.py:412
  40.8 23.8 %collective-permute-start.10 = (f32[384,256]{1,0:T(8,128)S(1)}, f32[384,256]{1,0:T(8,128)S(1)}, u32[]{:S(2)}, u32[]{:S(2)}) collective-permute-start(f32[384,256]{1,0:T(8,128)S(1)} %get-tuple-element.37.own), channel_id=1, source_target_pairs={{0,3},{1,2},{2,1},{3,0},{4,7},{5,6},{6,5},{7,4},{8,11},{9,10},{10,... | collective-permute-start | bytes 1179656 | tf_op jit(solution)/shard_map/ppermute | solution.py:412
  42.3 22.2 %collective-permute-start.5 = (f32[384,256]{1,0:T(8,128)S(1)}, f32[384,256]{1,0:T(8,128)S(1)}, u32[]{:S(2)}, u32[]{:S(2)}) collective-permute-start(f32[384,256]{1,0:T(8,128)S(1)} %get-tuple-element.37.own), channel_id=1, source_target_pairs={{0,1},{1,0},{2,3},{3,2},{4,5},{5,4},{6,7},{7,6},{8,9},{9,8},{10,11... | collective-permute-start | bytes 1179656 | tf_op jit(solution)/shard_map/ppermute | solution.py:412
  46.7 17.8 %collective-permute-start.9 = (f32[384,256]{1,0:T(8,128)S(1)}, f32[384,256]{1,0:T(8,128)S(1)}, u32[]{:S(2)}, u32[]{:S(2)}) collective-permute-start(f32[384,256]{1,0:T(8,128)S(1)} %get-tuple-element.37.own), channel_id=1, source_target_pairs={{0,2},{1,3},{2,0},{3,1},{4,6},{5,7},{6,4},{7,5},{8,10},{9,11},{10,... | collective-permute-start | bytes 1179656 | tf_op jit(solution)/shard_map/ppermute | solution.py:412
  47.4 1.3 %collective-permute-start.11 = (f32[64,256]{1,0:T(8,128)S(1)}, f32[64,256]{1,0:T(8,128)S(1)}, u32[]{:S(2)}, u32[]{:S(2)}) collective-permute-start(f32[64,256]{1,0:T(8,128)S(1)} %get-tuple-element.41.own), channel_id=1, source_target_pairs={{0,4},{4,0},{8,12},{12,8},{16,20},{20,16},{24,28},{28,24},{1,5},{5... | collective-permute-start | bytes 196616 | tf_op jit(solution)/shard_map/ppermute | solution.py:475
  49.3 4.3 %collective-permute-start.12 = (f32[64,256]{1,0:T(8,128)S(1)}, f32[64,256]{1,0:T(8,128)S(1)}, u32[]{:S(2)}, u32[]{:S(2)}) collective-permute-start(f32[64,256]{1,0:T(8,128)S(1)} %get-tuple-element.42.own), channel_id=1, source_target_pairs={{0,8},{4,12},{8,0},{12,4},{16,24},{20,28},{24,16},{28,20},{1,9},{5... | collective-permute-start | bytes 196616 | tf_op jit(solution)/shard_map/ppermute | solution.py:475
  54.2 8.9 %collective-permute-start.13 = (f32[64,256]{1,0:T(8,128)S(1)}, f32[64,256]{1,0:T(8,128)S(1)}, u32[]{:S(2)}, u32[]{:S(2)}) collective-permute-start(f32[64,256]{1,0:T(8,128)S(1)} %get-tuple-element.43.own), channel_id=1, source_target_pairs={{0,16},{4,20},{8,24},{12,28},{16,0},{20,4},{24,8},{28,12},{1,17},{... | collective-permute-start | bytes 196616 | tf_op jit(solution)/shard_map/ppermute | solution.py:475
